TPU v7x, 32 devices: a whole 2x2x4 slice. The times are simulated.
32 devices in a mesh: group: 4 (over y, core), ingroup: 8 (over z, x).
Axes of the slice: x: 2, y: 2, z: 4, core: 2. Of those that a mesh axis runs over, the one named last changes fastest.
Arguments:
- context: bfloat16 [512, 8192], P('group', 'ingroup'), may hold values from -6 to 6
- out_proj: bfloat16 [8192, 7168], P('ingroup'), may hold values from -0.0625 to 0.0625
- residual: bfloat16 [512, 7168], P(('group', 'ingroup')), may hold values from -6 to 6
- norm_gain: float32 [7168], replicated, may hold values from 0.25 to 1.75
- expert_ids: int32 [512, 8], P(('group', 'ingroup')), may hold values from 0 to 7, as said below
- gates: bfloat16 [512, 8], P(('group', 'ingroup')), may hold values from 0.099609375 to 1
- gate_proj: bfloat16 [32, 7168, 256], P(('group', 'ingroup')), may hold values from -0.0625 to 0.0625
- up_proj: bfloat16 [32, 7168, 256], P(('group', 'ingroup')), may hold values from -0.0625 to 0.0625
- down_proj: bfloat16 [32, 256, 7168], P(('group', 'ingroup')), may hold values from -0.1875 to 0.1875
Outputs:
- layer_out: bfloat16 [512, 7168], P(('group', 'ingroup'))
Inputs may be any that keep to these rules, and one draw needn't show every extreme that they name: `expert_ids`: each row names 8 different experts, all of them in at most 4 expert groups, expert e lying in group e // 2.
All inputs are finite; a program needn't handle non-finite values.
Results may differ from a plain program's by a relative error of at most 0.012.
Values may be sent and summed in bfloat16 or wider, within the bound.
A program may use at most 128 MiB of HBM per device.

v0:
```python
import jax
import jax.numpy as jnp
from jax import lax
from jax.sharding import PartitionSpec as P

TOPK = 8
SLICES = 4


def slice_output(arrived, gate_block, up_block, down_block):
    shape_in = arrived.shape
    flat_rows = arrived.reshape(-1, shape_in[-1])
    gate_part = jnp.dot(flat_rows, gate_block, preferred_element_type=jnp.float32)
    up_part = jnp.dot(flat_rows, up_block, preferred_element_type=jnp.float32)
    activated = (jax.nn.silu(gate_part) * up_part).astype(jnp.bfloat16)
    partial_out = jnp.dot(activated, down_block, preferred_element_type=jnp.float32).astype(
        jnp.bfloat16
    )
    return partial_out.reshape(shape_in[0], shape_in[1], down_block.shape[1])


def local(context, out_proj, residual, norm_gain, expert_ids, gates, gate_proj, up_proj, down_proj):
    group_count = lax.axis_size("group")
    member_count = lax.axis_size("ingroup")
    rows_here = residual.shape[0]
    model_width = residual.shape[1]
    local_experts = member_count // SLICES
    expert_total = group_count * local_experts
    capacity = min(rows_here, max(2, rows_here * TOPK * 5 // (4 * expert_total)))
    attended = lax.psum_scatter(
        jnp.dot(context, out_proj, preferred_element_type=jnp.float32),
        "ingroup",
        scatter_dimension=0,
        tiled=True,
    )
    hidden = (residual.astype(jnp.float32) + attended).astype(jnp.bfloat16)
    hidden_wide = hidden.astype(jnp.float32)
    inverse = lax.rsqrt(jnp.mean(hidden_wide * hidden_wide, axis=1, keepdims=True) + 1e-06)
    normed = (hidden_wide * inverse * norm_gain).astype(jnp.bfloat16)
    expert_iota = jnp.arange(expert_total, dtype=jnp.int32)
    matches = expert_ids[:, :, None] == expert_iota[None, None, :]
    picked = jnp.any(matches, axis=1)
    weighted = jnp.sum(
        jnp.where(matches, gates.astype(jnp.float32)[:, :, None], jnp.float32(0)), axis=1
    )
    gate_block = gate_proj[0]
    up_block = up_proj[0]
    down_block = down_proj[0]
    capacity_iota = jnp.arange(capacity, dtype=jnp.int32)
    picked_grid = picked.reshape(rows_here, group_count, local_experts)
    touched = jnp.any(picked_grid, axis=2).astype(jnp.int32)
    placed_at = jnp.cumsum(touched, axis=0) - touched
    slot_iota = jnp.arange(rows_here, dtype=jnp.int32)
    selector = (touched.T[:, None, :] > 0) & (placed_at.T[:, None, :] == slot_iota[None, :, None])
    selector_half = selector.astype(jnp.bfloat16)
    outgoing = jnp.einsum(
        "gst,td->gsd", selector_half, normed, preferred_element_type=jnp.float32
    ).astype(jnp.bfloat16)
    gate_grid = weighted.reshape(rows_here, group_count, local_experts).astype(jnp.bfloat16)
    outgoing_gates = jnp.einsum(
        "gst,tgl->gsl", selector_half, gate_grid, preferred_element_type=jnp.float32
    ).astype(jnp.bfloat16)
    arrived_rows, arrived_gates = (
        lax.all_to_all(outgoing, "group", split_axis=0, concat_axis=0, tiled=True),
        lax.all_to_all(outgoing_gates, "group", split_axis=0, concat_axis=0, tiled=True),
    )
    wanted = (arrived_gates > 0).astype(jnp.int32)
    relay_rank = jnp.cumsum(wanted, axis=1) - wanted
    relay_admit = (wanted > 0) & (relay_rank < capacity)
    admit_order = relay_admit.transpose(2, 0, 1)
    rank_order = relay_rank.transpose(2, 0, 1)
    placing = admit_order[:, :, None, :] & (
        rank_order[:, :, None, :] == capacity_iota[None, None, :, None]
    )
    placing_half = placing.astype(jnp.bfloat16)
    expert_rows = jnp.einsum(
        "lgcs,gsd->lgcd", placing_half, arrived_rows, preferred_element_type=jnp.float32
    ).astype(jnp.bfloat16)
    expert_rows = expert_rows.reshape(local_experts, group_count * capacity, model_width)
    dispatch = jnp.broadcast_to(
        expert_rows[:, None], (local_experts, SLICES, group_count * capacity, model_width)
    )
    dispatch = dispatch.reshape(member_count, group_count * capacity, model_width)
    returned = lax.all_to_all(
        slice_output(
            lax.all_to_all(dispatch, "ingroup", split_axis=0, concat_axis=0, tiled=True),
            gate_block,
            up_block,
            down_block,
        ),
        "ingroup",
        split_axis=0,
        concat_axis=0,
        tiled=True,
    )
    returned = returned.reshape(local_experts, SLICES, group_count, capacity, model_width)
    scaled = placing_half * arrived_gates.transpose(2, 0, 1)[:, :, None, :]
    group_out = jnp.einsum("lgcs,lugcd->gsd", scaled, returned, preferred_element_type=jnp.float32)
    back_home = lax.all_to_all(group_out, "group", split_axis=0, concat_axis=0, tiled=True)
    group_iota = jnp.arange(group_count, dtype=jnp.int32)
    fetched = back_home[group_iota[:, None], placed_at.T]
    mixture = jnp.sum(jnp.where(touched.T[:, :, None] > 0, fetched, jnp.float32(0)), axis=0)
    return (hidden_wide + mixture).astype(jnp.bfloat16)


def solution(mesh):
    in_specs = (
        P("group", "ingroup"),
        P("ingroup", None),
        P(("group", "ingroup"), None),
        P(),
        P(("group", "ingroup"), None),
        P(("group", "ingroup"), None),
        P(("group", "ingroup"), None, None),
        P(("group", "ingroup"), None, None),
        P(("group", "ingroup"), None, None),
    )
    out_specs = P(("group", "ingroup"), None)
    return jax.shard_map(local, mesh=mesh, in_specs=in_specs, out_specs=out_specs, check_vma=False)
```

profile of v0, /device:TPU:0, one launch (start us, length us, event | category | flops | bytes accessed | tf_op | source)
XLA Modules:
  0.0 514.3 jit_solution(13987403994483441625)
XLA Ops:
  6.5 0.9 copy-done
  7.5 9.1 %fusion.47 = f32[128,7168]{1,0:T(8,128)} fusion(bf16[128,1024]{1,0:T(8,128)(2,1)S(1)} %copy-done, bf16[1024,7168]{1,0:T(8,128)(2,1)} %param.10), kind=kOutput, calls=%fused_computation.60 | convolution fusion | flops 1879048192 | bytes 18612224 | tf_op jit(solution)/shard_map/dot_general | solution.py:31
  16.6 0.7 copy-done.5
  17.6 0.7 convolution_convert_fusion.3
  18.3 4.2 all-to-all-start
  22.6 78.1 %reduce-scatter.2.cloned.1.call-done = f32[16,7168]{1,0:T(8,128)} async-done(((f32[128,7168]{1,0:T(8,128)}), f32[16,7168]{1,0:T(8,128)}) %reduce-scatter.2.cloned.1.call-update) | async-done | bytes 458768 | tf_op jit(solution)/shard_map/reduce_scatter | solution.py:30
  100.7 1.2 fusion.16
  101.9 1.4 convolution_convert_fusion.2
  103.3 3.5 all-to-all-start.1
  107.1 12.7 %all-to-all-done.1 = bf16[4,16,7168]{2,1,0:T(8,128)(2,1)S(1)} async-done(((bf16[4,16,7168]{2,1,0:T(8,128)(2,1)}), bf16[4,16,7168]{2,1,0:T(8,128)(2,1)S(1)}, u32[]{:S(2)}, u32[]{:S(2)}) %all-to-all-start.1) | async-done | bytes 917536 | tf_op jit(solution)/shard_map/all_to_all | solution.py:64
  119.9 0.7 fusion
  120.8 1.0 broadcast_in_dim.32
  121.8 165.1 %all_to_all.25 = bf16[8,64,7168]{2,1,0:T(8,128)(2,1)S(1)} all-to-all(bf16[8,64,7168]{2,1,0:T(8,128)(2,1)S(1)} %bitcast.60), channel_id=1, replica_groups=mesh['group'=4,'ingroup'=8] {'ingroup'}, dimensions={0} | all-to-all | bytes 14680064 | tf_op jit(solution)/shard_map/all_to_all | solution.py:86
  286.9 3.0 copy-done.2
  289.9 2.1 fusion.4
  292.0 16.0 %convolution_convert_fusion = bf16[512,7168]{1,0:T(8,128)(2,1)} fusion(bf16[1,256,7168]{2,1,0:T(8,128)(2,1)} %param.17, bf16[512,7168]{1,0:T(8,128)(2,1)} %bitcast.58, bf16[1,7168,256]{2,1,0:T(8,128)(2,1)} %param.16, f32[512,256]{1,0:T(8,128)S(1)} %fusion.4), kind=kOutput, calls=%fused_computation.2 | convolution fusion | flops 3762552832 | bytes 22544384 | tf_op jit(solution)/shard_map/dot_general | solution.py:16
  308.0 163.9 %all_to_all.26 = bf16[8,64,7168]{2,1,0:T(8,128)(2,1)S(1)} all-to-all(bf16[8,64,7168]{2,1,0:T(8,128)(2,1)} %bitcast.59), channel_id=1, replica_groups=mesh['group'=4,'ingroup'=8] {'ingroup'}, dimensions={0} | all-to-all | bytes 14680064 | tf_op jit(solution)/shard_map/all_to_all | solution.py:84
  471.9 1.4 convert_reduce_fusion
  473.3 1.9 convolution_bitcast_fusion
  475.2 3.6 all-to-all-start.4
  479.0 22.7 %all-to-all-done.4 = f32[4,16,7168]{2,1,0:T(8,128)S(1)} async-done(((f32[4,16,7168]{2,1,0:T(8,128)}), f32[4,16,7168]{2,1,0:T(8,128)S(1)}, u32[]{:S(2)}, u32[]{:S(2)}) %all-to-all-start.4) | async-done | bytes 1835040 | tf_op jit(solution)/shard_map/all_to_all | solution.py:99
  501.6 3.3 gather_fusion
  505.0 1.8 select_reduce_fusion
  506.7 0.7 fusion.19
  (38 shorter events, 1.1 us)
Async XLA Ops:
  6.5 1.0 copy-start
  6.5 94.2 %reduce-scatter.2.cloned.1.call-start = ((), (), s32[]{:S(2)}) async-start(), calls=%async_computation.6 | async-start | bytes 4128768 | tf_op jit(solution)/shard_map/reduce_scatter | solution.py:30
  16.5 0.7 copy-start.5
  16.5 0.8 copy-start.6
  16.5 84.2 %copy-start.3 = (bf16[16,7168]{1,0:T(8,128)(2,1)S(1)}, bf16[16,7168]{1,0:T(8,128)(2,1)}, u32[]{:S(2)}) copy-start(bf16[16,7168]{1,0:T(8,128)(2,1)} %param.11) | copy-start | bytes 688132
  16.5 85.4 %copy-start.4 = (f32[7168]{0:T(1024)S(1)}, f32[7168]{0:T(1024)}, u32[]{:S(2)}) copy-start(f32[7168]{0:T(1024)} %param.12) | copy-start | bytes 86020
  18.3 85.0 %all-to-all-start = ((bf16[4,16,2]{1,2,0:T(2,128)(2,1)}), bf16[4,16,2]{1,2,0:T(2,128)(2,1)S(1)}, u32[]{:S(2)}, u32[]{:S(2)}) async-start(bf16[4,16,2]{1,2,0:T(2,128)(2,1)} %convolution_convert_fusion.3), calls=%async_computation.1 | async-start | bytes 4096 | tf_op jit(solution)/shard_map/all_to_all | solution.py:65
  103.3 16.5 %all-to-all-start.1 = ((bf16[4,16,7168]{2,1,0:T(8,128)(2,1)}), bf16[4,16,7168]{2,1,0:T(8,128)(2,1)S(1)}, u32[]{:S(2)}, u32[]{:S(2)}) async-start(bf16[4,16,7168]{2,1,0:T(8,128)(2,1)} %convolution_convert_fusion.2), calls=%async_computation.2 | async-start | bytes 1835008 | tf_op jit(solution)/shard_map/all_to_all | solution.py:64
  121.8 168.1 %copy-start.7 = (bf16[1,7168,256]{2,1,0:T(8,128)(2,1)S(1)}, bf16[1,7168,256]{2,1,0:T(8,128)(2,1)}, u32[]{:S(2)}) copy-start(bf16[1,7168,256]{2,1,0:T(8,128)(2,1)} %param.15) | copy-start | bytes 11010052
  286.9 3.0 copy-start.2
  475.2 26.4 %all-to-all-start.4 = ((f32[4,16,7168]{2,1,0:T(8,128)}), f32[4,16,7168]{2,1,0:T(8,128)S(1)}, u32[]{:S(2)}, u32[]{:S(2)}) async-start(f32[4,16,7168]{2,1,0:T(8,128)} %convolution_bitcast_fusion), calls=%async_computation.5 | async-start | bytes 3670016 | tf_op jit(solution)/shard_map/all_to_all | solution.py:99
  501.6 5.8 %copy-start.1 = (bf16[128,1024]{1,0:T(8,128)(2,1)S(1)}, bf16[128,1024]{1,0:T(8,128)(2,1)}, u32[]{:S(2)}) copy-start(bf16[128,1024]{1,0:T(8,128)(2,1)} %param.9) | copy-start | bytes 786436
Sparse Core Ops, SparseCore 0:
  16.7 83.9 reduce-scatter.1
where the time goes:
time: 515 us; the launch traced here: 514 us
  blocking collectives  329 us (64%)
  waiting for transfers between devices  114 us (22%)
  matrix products  31.9 us (6%)
  between operations  13.5 us (3%)
  starting transfers between devices  11.3 us (2%)
  local copies, waits for them, and re-layouts  9.76 us (2%)
  other arithmetic  5.32 us (1%)
    all_to_all x1, blocking collectives, local(): lax.all_to_all(dispatch, 'ingroup', split_axis=0, concat_axis=0, tiled=True)  165 us
    all_to_all x1, blocking collectives, local(): lax.all_to_all(slice_output(lax.all_to_all(dispatch, 'ingroup', split_axi...  164 us
    reduce_scatter x1, waiting for transfers between devices, local(): lax.psum_scatter(jnp.dot(context, out_proj, preferred_element_type=jnp.fl...  78.1 us
    all_to_all x1, waiting for transfers between devices, local(): lax.all_to_all(group_out, 'group', split_axis=0, concat_axis=0, tiled=True)  22.7 us
    dot_general x1, matrix products, slice_output(): jnp.dot(activated, down_block, preferred_element_type=jnp.float32)  16 us
    all_to_all x1, waiting for transfers between devices, local(): lax.all_to_all(outgoing, 'group', split_axis=0, concat_axis=0, tiled=True)  12.7 us
  transfers between devices with their start and end apart: 4, of which 3 were waited for; matrix products, arithmetic and copies ran while one was open for 1% of the time, Pallas kernels for 0%

commit v1 on v0

--- a/solution.py
+++ b/solution.py
@@ -1,6 +1,10 @@
+import functools
+
 import jax
 import jax.numpy as jnp
 from jax import lax
+from jax.experimental import pallas as pl
+from jax.experimental.pallas import tpu as pltpu
 from jax.sharding import PartitionSpec as P
 
 TOPK = 8
@@ -103,6 +107,420 @@
     return (hidden_wide + mixture).astype(jnp.bfloat16)
 
 
+SIDE = 2
+DEPTH = 4
+CHUNKS = 4
+OFFSETS = (0, 1, -1, 2, -2, 3, -3)
+MESH = pl.DeviceIdType.MESH
+BF16 = jnp.bfloat16
+F32 = jnp.float32
+
+
+class Place:
+    def __init__(self):
+        group, member = lax.axis_index("group"), lax.axis_index("ingroup")
+        self.y, self.c = lax.div(group, 2), lax.rem(group, 2)
+        self.z, self.x = lax.div(member, SIDE), lax.rem(member, SIDE)
+        self.xo, self.yo, self.co = 1 - self.x, 1 - self.y, 1 - self.c
+        self.at_x = {"group": group, "ingroup": self.z * SIDE + self.xo}
+        self.at_y = {"group": self.yo * 2 + self.c, "ingroup": member}
+        self.at_core = {"group": self.y * 2 + self.co, "ingroup": member}
+
+    def at_z(self, step):
+        z = lax.rem(self.z + step + DEPTH, DEPTH)
+        return {"group": self.y * 2 + self.c, "ingroup": z * SIDE + self.x}
+
+    def has_z(self, offset):
+        return jnp.logical_and(self.z + offset >= 0, self.z + offset < DEPTH)
+
+    def meet(self):
+        barrier = pltpu.get_barrier_semaphore()
+        for device in (self.at_x, self.at_y, self.at_core, self.at_z(1), self.at_z(-1)):
+            pl.semaphore_signal(barrier, inc=1, device_id=device, device_id_type=MESH)
+        pl.semaphore_wait(barrier, 5)
+
+
+def remote(source, target, send, recv, device):
+    return pltpu.make_async_remote_copy(
+        src_ref=source, dst_ref=target, send_sem=send, recv_sem=recv, device_id=device,
+        device_id_type=MESH,
+    )
+
+
+def chain_z(place, sums, slots, send, recv, columns, order=(3, 2, 1)):
+    z = place.z
+    for k in order:
+        for way, step in enumerate((1, -1)):
+            @pl.when(place.has_z(step * k))
+            def _():
+                block = sums.at[z + step * k, :, columns]
+                if k < DEPTH - 1:
+                    @pl.when(place.has_z(-step))
+                    def _():
+                        landed = slots.at[way, k, :, columns]
+                        remote(landed, landed, send.at[way, k], recv.at[way, k], place.at_z(step)).wait_recv()
+                        block[...] = (block[...].astype(F32) + landed[...].astype(F32)).astype(BF16)
+                remote(
+                    block, slots.at[way, k - 1, :, columns], send.at[way, k - 1], recv.at[way, k - 1],
+                    place.at_z(step),
+                ).start()
+
+
+def chain_z_end(place, slots, total, send, recv, columns):
+    for way, step in enumerate((1, -1)):
+        @pl.when(place.has_z(-step))
+        def _():
+            landed = slots.at[way, 0, :, columns]
+            remote(landed, landed, send.at[way, 0], recv.at[way, 0], place.at_z(step)).wait_recv()
+            total[:, columns] += landed[...].astype(F32)
+
+
+def chain_z_sent(place, sums, slots, send, recv, columns):
+    for k in (3, 2, 1):
+        for way, step in enumerate((1, -1)):
+            @pl.when(place.has_z(step * k))
+            def _():
+                remote(
+                    sums.at[place.z + step * k, :, columns], slots.at[way, k - 1, :, columns],
+                    send.at[way, k - 1], recv.at[way, k - 1], place.at_z(step),
+                ).wait_send()
+
+
+def spread_kernel(
+    part, residual, gain, hidden, rows_out,
+    x_slots, sums, z_slots, total,
+    x_send, x_recv, z_send, z_recv,
+    a_send, a_recv, b_send, b_recv, d_send, d_recv, c_send, c_recv,
+):
+    place = Place()
+    width = residual.shape[1]
+    chunk = width // CHUNKS
+    place.meet()
+    cuts = [pl.ds(i * chunk, chunk) for i in range(CHUNKS)]
+
+    def x_copy(i):
+        return remote(
+            part.at[:, place.xo, :, cuts[i]], x_slots.at[:, :, cuts[i]], x_send.at[i], x_recv.at[i],
+            place.at_x,
+        )
+
+    for i in range(CHUNKS):
+        x_copy(i).start()
+    for i in range(CHUNKS):
+        x_copy(i).wait_recv()
+        for d in range(DEPTH):
+            sums[d, :, cuts[i]] = (
+                part[d, place.x, :, cuts[i]].astype(F32) + x_slots[d, :, cuts[i]].astype(F32)
+            ).astype(BF16)
+        total[:, cuts[i]] = residual[:, cuts[i]].astype(F32) + sums[place.z, :, cuts[i]].astype(F32)
+        chain_z(place, sums, z_slots, z_send.at[i], z_recv.at[i], cuts[i])
+    for i in range(CHUNKS):
+        chain_z_end(place, z_slots, total, z_send.at[i], z_recv.at[i], cuts[i])
+    hidden[...] = total[...].astype(BF16)
+    wide = hidden[...].astype(F32)
+    inverse = lax.rsqrt(jnp.mean(wide * wide, axis=1, keepdims=True) + 1e-06)
+
+    def index(y, c, z, x):
+        return ((y * 2 + c) * DEPTH + z) * SIDE + x
+
+    x, y, z, c = place.x, place.y, place.z, place.c
+    half = width // 2
+    cut_a, cut_b = pl.ds(0, half), pl.ds(half, half)
+    rows_out[index(y, c, z, x)] = (wide * inverse * gain[...]).astype(BF16)
+
+    def here(i, by_x, by_y):
+        return index(place.yo if by_y else y, c, z - OFFSETS[i], place.xo if by_x else x)
+
+    def copy_to(device, block, columns, send, recv):
+        ref = rows_out.at[block, :, columns]
+        return remote(ref, ref, send, recv, device)
+
+    whole = pl.ds(0, width)
+
+    def z_copy(i, step):
+        there = OFFSETS.index(OFFSETS[i] + step)
+        return copy_to(
+            place.at_z(step), here(i, False, False), whole, a_send.at[there], a_recv.at[there]
+        )
+
+    def z_steps(i):
+        offset = OFFSETS[i]
+        return [s for s in (1, -1) if offset * s >= 0 and abs(offset + s) < DEPTH]
+
+    def x_full(i):
+        return copy_to(place.at_x, here(i, False, False), whole, b_send.at[i, 0], b_recv.at[i, 0])
+
+    def y_full(i):
+        return copy_to(place.at_y, here(i, False, False), whole, b_send.at[i, 1], b_recv.at[i, 1])
+
+    def y_half(i):
+        return copy_to(place.at_y, here(i, True, False), cut_a, d_send.at[i, 0], d_recv.at[i, 0])
+
+    def x_half(i):
+        return copy_to(place.at_x, here(i, False, True), cut_b, d_send.at[i, 1], d_recv.at[i, 1])
+
+    def core_copy(i, by_x, by_y):
+        k = by_x * 2 + by_y
+        return copy_to(
+            place.at_core, here(i, by_x, by_y), whole, c_send.at[i, k], c_recv.at[i, k]
+        )
+
+    def along_z(i):
+        @pl.when(place.has_z(-OFFSETS[i]))
+        def _():
+            if i > 0:
+                copy_to(place.at_x, here(i, False, False), whole, a_send.at[i], a_recv.at[i]).wait_recv()
+            for step in z_steps(i):
+                @pl.when(place.has_z(step))
+                def _():
+                    z_copy(i, step).start()
+            x_full(i).start()
+            y_full(i).start()
+            core_copy(i, 0, 0).start()
+
+    def along_xy(i):
+        @pl.when(place.has_z(-OFFSETS[i]))
+        def _():
+            copy_to(place.at_x, here(i, True, False), whole, b_send.at[i, 0], b_recv.at[i, 0]).wait_recv()
+            y_half(i).start()
+            core_copy(i, 1, 0).start()
+            copy_to(place.at_x, here(i, False, True), whole, b_send.at[i, 1], b_recv.at[i, 1]).wait_recv()
+            x_half(i).start()
+            core_copy(i, 0, 1).start()
+
+    def along_diagonal(i):
+        @pl.when(place.has_z(-OFFSETS[i]))
+        def _():
+            for k, columns in enumerate((cut_a, cut_b)):
+                copy_to(
+                    place.at_x, here(i, True, True), columns, d_send.at[i, k], d_recv.at[i, k]
+                ).wait_recv()
+            core_copy(i, 1, 1).start()
+
+    near = ((0,), (1, 2), (3, 4), (5, 6))
+    for t in range(DEPTH + 2):
+        for i in near[t] if t < DEPTH else ():
+            along_z(i)
+        for i in near[t - 1] if 0 <= t - 1 < DEPTH else ():
+            along_xy(i)
+        for i in near[t - 2] if 0 <= t - 2 < DEPTH else ():
+            along_diagonal(i)
+    for i in range(len(OFFSETS)):
+        @pl.when(place.has_z(-OFFSETS[i]))
+        def _():
+            for step in z_steps(i):
+                @pl.when(place.has_z(step))
+                def _():
+                    z_copy(i, step).wait_send()
+            for copy in (x_full(i), y_full(i), x_half(i), y_half(i)):
+                copy.wait_send()
+            for by_x in (0, 1):
+                for by_y in (0, 1):
+                    core_copy(i, by_x, by_y).wait_send()
+                    block = index(
+                        place.yo if by_y else y, place.co, z - OFFSETS[i], place.xo if by_x else x
+                    )
+                    copy_to(
+                        place.at_core, block, whole, c_send.at[i, by_x * 2 + by_y],
+                        c_recv.at[i, by_x * 2 + by_y],
+                    ).wait_recv()
+    for i in range(CHUNKS):
+        x_copy(i).wait_send()
+        chain_z_sent(place, sums, z_slots, z_send.at[i], z_recv.at[i], cuts[i])
+
+
+def gather_sum_kernel(
+    parts, mixture,
+    core_slots, sums, a_slots, b_slots, x_slots, y_slots, own, z_slots,
+    c_send, c_recv, d_send, d_recv, f_send, f_recv, z_send, z_recv,
+):
+    place = Place()
+    width = mixture.shape[1]
+    half = width // 2
+    cut_a, cut_b, whole = pl.ds(0, half), pl.ds(half, half), pl.ds(0, width)
+    x, y, z, xo, yo = place.x, place.y, place.z, place.xo, place.yo
+    place.meet()
+    far = (6, 5, 4, 3, 2, 1, 0)
+
+    def core_copy(i):
+        d = z - OFFSETS[i]
+        return remote(
+            parts.at[:, place.co, d], core_slots.at[d], c_send.at[i], c_recv.at[i], place.at_core
+        )
+
+    def diagonal_a(i):
+        d = z - OFFSETS[i]
+        return remote(
+            sums.at[d, yo, xo, :, cut_a], a_slots.at[d], d_send.at[i, 0], d_recv.at[i, 0], place.at_y
+        )
+
+    def diagonal_b(i):
+        d = z - OFFSETS[i]
+        return remote(
+            sums.at[d, yo, xo, :, cut_b], b_slots.at[d], d_send.at[i, 1], d_recv.at[i, 1], place.at_x
+        )
+
+    def full_x(i):
+        d = z - OFFSETS[i]
+        return remote(sums.at[d, y, xo], x_slots.at[d], f_send.at[i, 0], f_recv.at[i, 0], place.at_x)
+
+    def full_y(i):
+        d = z - OFFSETS[i]
+        return remote(sums.at[d, yo, x], y_slots.at[d], f_send.at[i, 1], f_recv.at[i, 1], place.at_y)
+
+    def each(i, body):
+        pl.when(place.has_z(-OFFSETS[i]))(body)
+
+    def first(i):
+        def body():
+            d = z - OFFSETS[i]
+            core_copy(i).wait_recv()
+            for j in (yo, y):
+                for k in (xo, x):
+                    sums[d, j, k] = (
+                        parts[j, place.c, d, k].astype(F32) + core_slots[d, j, k].astype(F32)
+                    ).astype(BF16)
+                if j is yo:
+                    diagonal_a(i).start()
+                    diagonal_b(i).start()
+
+        each(i, body)
+
+    def second(i):
+        def body():
+            d = z - OFFSETS[i]
+            diagonal_a(i).wait_recv()
+            sums[d, y, xo, :, cut_a] = (
+                sums[d, y, xo, :, cut_a].astype(F32) + a_slots[d].astype(F32)
+            ).astype(BF16)
+            full_x(i).start()
+            diagonal_b(i).wait_recv()
+            sums[d, yo, x, :, cut_b] = (
+                sums[d, yo, x, :, cut_b].astype(F32) + b_slots[d].astype(F32)
+            ).astype(BF16)
+            full_y(i).start()
+
+        each(i, body)
+
+    def third(i):
+        def body():
+            d = z - OFFSETS[i]
+            full_x(i).wait_recv()
+            full_y(i).wait_recv()
+            own[d] = (
+                sums[d, y, x].astype(F32) + x_slots[d].astype(F32) + y_slots[d].astype(F32)
+            ).astype(BF16)
+
+        each(i, body)
+
+    levels = ((6, 5), (4, 3), (2, 1), (0,))
+    for i in far:
+        each(i, lambda i=i: core_copy(i).start())
+    for t in range(len(levels) + 2):
+        for i in levels[t] if t < len(levels) else ():
+            first(i)
+        for i in levels[t - 1] if 0 <= t - 1 < len(levels) else ():
+            second(i)
+        if 0 <= t - 2 < len(levels):
+            for i in levels[t - 2]:
+                third(i)
+            if t - 2 < DEPTH - 1:
+                chain_z(place, own, z_slots, z_send, z_recv, whole, order=(DEPTH - 1 - (t - 2),))
+    mixture[...] = own[z].astype(F32)
+    chain_z_end(place, z_slots, mixture, z_send, z_recv, whole)
+    for i in far:
+        def body(i=i):
+            for copy in (core_copy(i), diagonal_a(i), diagonal_b(i), full_x(i), full_y(i)):
+                copy.wait_send()
+
+        each(i, body)
+    chain_z_sent(place, own, z_slots, z_send, z_recv, whole)
+
+
+def local_dense(
+    context, out_proj, residual, norm_gain, expert_ids, gates, gate_proj, up_proj, down_proj
+):
+    group_count = lax.axis_size("group")
+    member_count = lax.axis_size("ingroup")
+    devices = group_count * member_count
+    rows, width = residual.shape
+    local_experts = member_count // SLICES
+    expert_total = group_count * local_experts
+    capacity = min(rows, max(2, rows * TOPK * 5 // (4 * expert_total)))
+    offsets = len(OFFSETS)
+    dma = pltpu.SemaphoreType.DMA
+    vmem = pl.BlockSpec(memory_space=pltpu.VMEM)
+
+    matches = expert_ids[:, :, None] == jnp.arange(expert_total, dtype=jnp.int32)[None, None, :]
+    picked = jnp.any(matches, axis=1).astype(jnp.int32)
+    ranking = jnp.cumsum(picked, axis=0) - picked
+    weighted = jnp.sum(jnp.where(matches, gates.astype(F32)[:, :, None], F32(0)), axis=1)
+    weighted = jnp.where((picked > 0) & (ranking < capacity), weighted, F32(0)).astype(BF16)
+    weights = lax.all_gather(weighted, ("group", "ingroup"), axis=0, tiled=True)
+
+    part = jnp.dot(context, out_proj, preferred_element_type=F32).astype(BF16)
+    hidden, normed = pl.pallas_call(
+        spread_kernel,
+        out_shape=(
+            jax.ShapeDtypeStruct((rows, width), BF16),
+            jax.ShapeDtypeStruct((devices, rows, width), BF16),
+        ),
+        in_specs=[vmem] * 3,
+        out_specs=(vmem, vmem),
+        scratch_shapes=[
+            pltpu.VMEM((DEPTH, rows, width), BF16),
+            pltpu.VMEM((DEPTH, rows, width), BF16),
+            pltpu.VMEM((2, DEPTH - 1, rows, width), BF16),
+            pltpu.VMEM((rows, width), F32),
+            dma((CHUNKS,)), dma((CHUNKS,)),
+            dma((CHUNKS, 2, DEPTH - 1)), dma((CHUNKS, 2, DEPTH - 1)),
+            dma((offsets,)), dma((offsets,)),
+            dma((offsets, 2)), dma((offsets, 2)),
+            dma((offsets, 2)), dma((offsets, 2)),
+            dma((offsets, 4)), dma((offsets, 4)),
+        ],
+        compiler_params=pltpu.CompilerParams(
+            collective_id=0, has_side_effects=True, vmem_limit_bytes=48 * 2**20
+        ),
+        name="spread",
+    )(part.reshape(DEPTH, SIDE, rows, width), residual, norm_gain.reshape(1, width))
+
+    flat = normed.reshape(devices * rows, width)
+    gate_part = jnp.dot(flat, gate_proj[0], preferred_element_type=F32)
+    up_part = jnp.dot(flat, up_proj[0], preferred_element_type=F32)
+    activated = (jax.nn.silu(gate_part) * up_part).astype(BF16)
+    parts = jnp.dot(activated, down_proj[0], preferred_element_type=F32)
+    expert = lax.axis_index("group") * local_experts + lax.axis_index("ingroup") // SLICES
+    weight = lax.dynamic_slice_in_dim(weights, expert, 1, axis=1).astype(F32)
+    parts = (parts * weight).astype(BF16)
+
+    mixture = pl.pallas_call(
+        gather_sum_kernel,
+        out_shape=jax.ShapeDtypeStruct((rows, width), F32),
+        in_specs=[vmem],
+        out_specs=vmem,
+        scratch_shapes=[
+            pltpu.VMEM((DEPTH, SIDE, SIDE, rows, width), BF16),
+            pltpu.VMEM((DEPTH, SIDE, SIDE, rows, width), BF16),
+            pltpu.VMEM((DEPTH, rows, width // 2), BF16),
+            pltpu.VMEM((DEPTH, rows, width // 2), BF16),
+            pltpu.VMEM((DEPTH, rows, width), BF16),
+            pltpu.VMEM((DEPTH, rows, width), BF16),
+            pltpu.VMEM((DEPTH, rows, width), BF16),
+            pltpu.VMEM((2, DEPTH - 1, rows, width), BF16),
+            dma((offsets,)), dma((offsets,)),
+            dma((offsets, 2)), dma((offsets, 2)),
+            dma((offsets, 2)), dma((offsets, 2)),
+            dma((2, DEPTH - 1)), dma((2, DEPTH - 1)),
+        ],
+        compiler_params=pltpu.CompilerParams(
+            collective_id=1, has_side_effects=True, vmem_limit_bytes=48 * 2**20
+        ),
+        name="gather_sum",
+    )(parts.reshape(SIDE, 2, DEPTH, SIDE, rows, width))
+    return (hidden.astype(F32) + mixture).astype(BF16)
+
+
 def solution(mesh):
     in_specs = (
         P("group", "ingroup"),
@@ -116,4 +534,6 @@
         P(("group", "ingroup"), None, None),
     )
     out_specs = P(("group", "ingroup"), None)
-    return jax.shard_map(local, mesh=mesh, in_specs=in_specs, out_specs=out_specs, check_vma=False)
+    sizes = (mesh.shape["group"], mesh.shape["ingroup"])
+    body = local_dense if sizes == (2 * SIDE, SIDE * DEPTH) else local
+    return jax.shard_map(body, mesh=mesh, in_specs=in_specs, out_specs=out_specs, check_vma=False)

time: 515 us -> 212 us (0.41)
  blocking collectives: 329 us -> 70 us
  waiting for transfers between devices: 114 us -> 0 us
  Pallas kernels: 0 us -> 110 us
  between operations: 13.5 us -> 0.11 us
  starting transfers between devices: 11.3 us -> 0 us
  local copies, waits for them, and re-layouts: 9.76 us -> 0.31 us
    all_to_all x2 -> x0, blocking collectives: 329 us -> none  [the longest x1 165 us: local(): lax.all_to_all(dispatch, 'ingroup', split_axis=0, concat_axis=0, tiled=True)]
    pallas_call x0 -> x2, Pallas kernels: none -> 110 us  [the longest x1 70.1 us: local_dense(): pl.pallas_call(spread_kernel, out_shape=(jax.ShapeDtypeStruct((rows, widt...]
    reduce_scatter x1 -> x0, waiting for transfers between devices: 78.1 us -> none  [local(): lax.psum_scatter(jnp.dot(context, out_proj, preferred_element_type=jnp.fl...]
    all_gather x0 -> x1, blocking collectives: none -> 70 us  [local_dense(): weights = lax.all_gather(weighted, ('group', 'ingroup'), axis=0, tiled=True)]
    all_to_all x3 -> x0, waiting for transfers between devices: 35.4 us -> none  [the longest x1 22.7 us: local(): lax.all_to_all(group_out, 'group', split_axis=0, concat_axis=0, tiled=True)]
    all_to_all x3 -> x0, starting transfers between devices: 11.3 us -> none  [the longest x1 4.24 us: local(): lax.all_to_all(outgoing_gates, 'group', split_axis=0, concat_axis=0, tile...]
    dot_general x7 -> x3, matrix products: 31.9 us -> 28.6 us  [the longest x1 16 us: local_dense(): parts = jnp.dot(activated, down_proj[0], preferred_element_type=F32)]
  transfers between devices with their start and end apart: 4 -> 0, of which waited for: 3 -> 0; matrix products, arithmetic and copies ran while one was open for 1% -> 0% of each run, Pallas kernels for 0% -> 0%
where the time goes in v1:
time: 212 us; the launch traced here: 211 us
  Pallas kernels  110 us (52%)
  blocking collectives  70 us (33%)
  matrix products  28.6 us (13%)
  other arithmetic  2.93 us (1%)
    pallas_call x1, Pallas kernels, local_dense(): pl.pallas_call(spread_kernel, out_shape=(jax.ShapeDtypeStruct((rows, widt...  70.1 us
    all_gather x1, blocking collectives, local_dense(): weights = lax.all_gather(weighted, ('group', 'ingroup'), axis=0, tiled=True)  70 us
    pallas_call x1, Pallas kernels, local_dense(): pl.pallas_call(gather_sum_kernel, out_shape=jax.ShapeDtypeStruct((rows, w...  39.5 us
    dot_general x1, matrix products, local_dense(): parts = jnp.dot(activated, down_proj[0], preferred_element_type=F32)  16 us
    dot_general x1, matrix products, local_dense(): part = jnp.dot(context, out_proj, preferred_element_type=F32).astype(BF16)  7.41 us
    dot_general x1, matrix products, local_dense(): gate_part = jnp.dot(flat, gate_proj[0], preferred_element_type=F32)  5.14 us

profile of v1, /device:TPU:0, one launch (start us, length us, event | category | flops | bytes accessed | tf_op | source)
XLA Modules:
  0.0 211.5 jit_solution(12695177765671199561)
XLA Ops:
  0.0 0.0 copy-start
  0.0 0.7 fusion.14
  0.8 0.1 copy.25
  0.9 0.1 copy.26
  0.9 0.7 convert_element_type.29
  1.6 0.7 select_reduce_fusion
  2.3 70.0 %all-gather = bf16[32,16,8]{1,2,0:T(8,128)(2,1)S(1)} all-gather(bf16[1,16,8]{1,2,0:T(8,128)(2,1)S(1)} %fusion.16), channel_id=1, replica_groups=mesh['group'=4,'ingroup'=8] {'group','ingroup'}, dimensions={0}, use_global_device_ids=true | all-gather | bytes 8448 | tf_op jit(solution)/shard_map/all_gather | solution.py:459
  72.3 0.1 reshape.20
  72.5 0.0 copy-done
  72.5 0.0 copy-start.1
  72.5 0.0 copy-start.2
  72.5 0.0 copy-start.3
  72.5 7.4 %convolution_convert_fusion = bf16[128,7168]{1,0:T(8,128)(2,1)S(1)} fusion(bf16[128,1024]{1,0:T(8,128)(2,1)S(1)} %copy-done, bf16[1024,7168]{1,0:T(8,128)(2,1)} %param.10), kind=kOutput, calls=%fused_computation.1 | convolution fusion | flops 1879965696 | bytes 16777216 | tf_op jit(solution)/shard_map/dot_general | solution.py:461
  79.9 0.0 copy-done.1
  80.0 0.0 copy-done.2
  80.0 70.1 %spread.1 = (bf16[16,7168]{1,0:T(8,128)(2,1)S(1)}, bf16[32,16,7168]{2,1,0:T(8,128)(2,1)}) custom-call(bf16[4,2,16,7168]{3,2,1,0:T(8,128)(2,1)S(1)} %bitcast.28, bf16[16,7168]{1,0:T(8,128)(2,1)S(1)} %copy-done.1, f32[1,7168]{1,0:T(1,128)S(1)} %bitcast.29), custom_call_target="tpu_custom_call" | custom-call | tf_op jit(solution)/shard_map/spread/pallas_call | solution.py:462
  150.1 0.0 copy-done.3
  150.1 5.1 %fusion.3 = f32[512,256]{1,0:T(8,128)S(1)} fusion(bf16[512,7168]{1,0:T(8,128)(2,1)} %bitcast.32, bf16[1,7168,256]{2,1,0:T(8,128)(2,1)S(1)} %copy-done.3), kind=kOutput, calls=%fused_computation.5 | convolution fusion | flops 1879048192 | bytes 11534336 | tf_op jit(solution)/shard_map/dot_general | solution.py:489
  155.3 16.0 %multiply_convert_fusion = bf16[512,7168]{1,0:T(8,128)(2,1)} fusion(f32[512]{0:T(512)S(1)} %bitcast.31, bf16[1,256,7168]{2,1,0:T(8,128)(2,1)} %param.17, bf16[512,7168]{1,0:T(8,128)(2,1)} %bitcast.33, bf16[1,7168,256]{2,1,0:T(8,128)(2,1)} %param.16, f32[512,256]{1,0:T(8,128)S(1)} %fusion.3), kind=kOutput, calls=%fused_computation | convolution fusion | flops 3766222848 | bytes 22546432 | tf_op jit(solution)/shard_map/dot_general | solution.py:492
  171.3 39.5 %gather_sum.1 = f32[16,7168]{1,0:T(8,128)S(1)} custom-call(bf16[2,2,4,2,16,7168]{5,4,3,2,1,0:T(8,128)(2,1)} %bitcast.30), custom_call_target="tpu_custom_call" | custom-call | tf_op jit(solution)/shard_map/gather_sum/pallas_call | solution.py:497
  210.7 0.7 add_convert_fusion
  (5 shorter events, 0.1 us)
Async XLA Ops:
  0.0 72.5 %copy-start = (bf16[128,1024]{1,0:T(8,128)(2,1)S(1)}, bf16[128,1024]{1,0:T(8,128)(2,1)}, u32[]{:S(2)}) copy-start(bf16[128,1024]{1,0:T(8,128)(2,1)} %param.9) | copy-start | bytes 786436
  72.5 7.5 %copy-start.1 = (bf16[16,7168]{1,0:T(8,128)(2,1)S(1)}, bf16[16,7168]{1,0:T(8,128)(2,1)}, u32[]{:S(2)}) copy-start(bf16[16,7168]{1,0:T(8,128)(2,1)} %residual.1) | copy-start | bytes 688132
  72.5 7.4 %copy-start.2 = (f32[7168]{0:T(1024)S(1)}, f32[7168]{0:T(1024)}, u32[]{:S(2)}) copy-start(f32[7168]{0:T(1024)} %param.12) | copy-start | bytes 86020
  72.5 77.6 %copy-start.3 = (bf16[1,7168,256]{2,1,0:T(8,128)(2,1)S(1)}, bf16[1,7168,256]{2,1,0:T(8,128)(2,1)}, u32[]{:S(2)}) copy-start(bf16[1,7168,256]{2,1,0:T(8,128)(2,1)} %param.15) | copy-start | bytes 11010052

commit v2 on v0

--- a/solution.py
+++ b/solution.py
@@ -1,6 +1,10 @@
+import functools
+
 import jax
 import jax.numpy as jnp
 from jax import lax
+from jax.experimental import pallas as pl
+from jax.experimental.pallas import tpu as pltpu
 from jax.sharding import PartitionSpec as P
 
 TOPK = 8
@@ -103,6 +107,520 @@
     return (hidden_wide + mixture).astype(jnp.bfloat16)
 
 
+SIDE = 2
+DEPTH = 4
+CHUNKS = 4
+PASSES = 2
+SIDE_COLUMNS = 128
+OFFSETS = (0, 1, -1, 2, -2, 3, -3)
+MESH = pl.DeviceIdType.MESH
+BF16 = jnp.bfloat16
+F32 = jnp.float32
+
+
+class Place:
+    def __init__(self):
+        group, member = lax.axis_index("group"), lax.axis_index("ingroup")
+        self.y, self.c = lax.div(group, 2), lax.rem(group, 2)
+        self.z, self.x = lax.div(member, SIDE), lax.rem(member, SIDE)
+        self.xo, self.yo, self.co = 1 - self.x, 1 - self.y, 1 - self.c
+        self.at_x = {"group": group, "ingroup": self.z * SIDE + self.xo}
+        self.at_y = {"group": self.yo * 2 + self.c, "ingroup": member}
+        self.at_core = {"group": self.y * 2 + self.co, "ingroup": member}
+
+    def at_z(self, step):
+        z = lax.rem(self.z + step + DEPTH, DEPTH)
+        return {"group": self.y * 2 + self.c, "ingroup": z * SIDE + self.x}
+
+    def has_z(self, offset):
+        return jnp.logical_and(self.z + offset >= 0, self.z + offset < DEPTH)
+
+    def meet(self):
+        barrier = pltpu.get_barrier_semaphore()
+        for device in (self.at_x, self.at_y, self.at_core, self.at_z(1), self.at_z(-1)):
+            pl.semaphore_signal(barrier, inc=1, device_id=device, device_id_type=MESH)
+        pl.semaphore_wait(barrier, 5)
+
+
+def remote(source, target, send, recv, device):
+    return pltpu.make_async_remote_copy(
+        src_ref=source, dst_ref=target, send_sem=send, recv_sem=recv, device_id=device,
+        device_id_type=MESH,
+    )
+
+
+def chain_z(place, sums, slots, send, recv, columns, order=(3, 2, 1)):
+    z = place.z
+    for k in order:
+        for way, step in enumerate((1, -1)):
+            @pl.when(place.has_z(step * k))
+            def _():
+                block = sums.at[z + step * k, :, columns]
+                if k < DEPTH - 1:
+                    @pl.when(place.has_z(-step))
+                    def _():
+                        landed = slots.at[way, k, :, columns]
+                        remote(landed, landed, send.at[way, k], recv.at[way, k], place.at_z(step)).wait_recv()
+                        block[...] = (block[...].astype(F32) + landed[...].astype(F32)).astype(BF16)
+                remote(
+                    block, slots.at[way, k - 1, :, columns], send.at[way, k - 1], recv.at[way, k - 1],
+                    place.at_z(step),
+                ).start()
+
+
+def chain_z_end(place, slots, total, send, recv, columns):
+    for way, step in enumerate((1, -1)):
+        @pl.when(place.has_z(-step))
+        def _():
+            landed = slots.at[way, 0, :, columns]
+            remote(landed, landed, send.at[way, 0], recv.at[way, 0], place.at_z(step)).wait_recv()
+            total[:, columns] += landed[...].astype(F32)
+
+
+def chain_z_sent(place, sums, slots, send, recv, columns):
+    for k in (3, 2, 1):
+        for way, step in enumerate((1, -1)):
+            @pl.when(place.has_z(step * k))
+            def _():
+                remote(
+                    sums.at[place.z + step * k, :, columns], slots.at[way, k - 1, :, columns],
+                    send.at[way, k - 1], recv.at[way, k - 1], place.at_z(step),
+                ).wait_send()
+
+
+def layer_kernel(
+    context, out_proj, residual, gain, weighted, gate_proj, up_proj, down_proj, out,
+    proj, gate, up, down, part, x_slots, sums, z_slots, total, hidden, rows, act, parts,
+    core_slots, sums2, a_slots, b_slots, x_slots2, y_slots2, own, z_slots2,
+    w_sem, proj_sem, x_send, x_recv, z_send, z_recv,
+    a_send, a_recv, b_send, b_recv, d_send, d_recv, c_send, c_recv,
+    core_send, core_recv, e_send, e_recv, f_send, f_recv, z2_send, z2_recv,
+):
+    place = Place()
+    x, y, z, c, xo, yo, co = place.x, place.y, place.z, place.c, place.xo, place.yo, place.co
+    rows_here, width = residual.shape
+    chunk = width // CHUNKS
+    span = width // PASSES
+    block_rows = rows_here * SIDE * 2 * DEPTH
+    cuts = [pl.ds(i * chunk, chunk) for i in range(CHUNKS)]
+    extra = pl.ds(width, SIDE_COLUMNS)
+    passes = [pl.ds(0, span), pl.ds(span, span + SIDE_COLUMNS)]
+
+    def each(i, body):
+        pl.when(place.has_z(-OFFSETS[i]))(body)
+
+    def proj_copy(i):
+        return pltpu.make_async_copy(out_proj.at[:, cuts[i]], proj.at[i % 2], proj_sem.at[i])
+
+    weight_copies = [
+        pltpu.make_async_copy(source.at[0], target, w_sem.at[i])
+        for i, (source, target) in enumerate(((gate_proj, gate), (up_proj, up), (down_proj, down)))
+    ]
+    proj_copy(0).start()
+    proj_copy(1).start()
+    place.meet()
+
+    def x_copy(i):
+        return remote(
+            part.at[:, xo, :, cuts[i]], x_slots.at[:, :, cuts[i]], x_send.at[i], x_recv.at[i], place.at_x
+        )
+
+    tile = 256
+    for i in range(CHUNKS):
+        proj_copy(i).wait()
+
+        def multiply(t, carry, i=i):
+            inside = pl.ds(pl.multiple_of(t * tile, tile), tile)
+            columns = pl.ds(pl.multiple_of(t * tile + i * chunk, tile), tile)
+            product = jnp.dot(context[...], proj[i % 2, :, inside], preferred_element_type=F32)
+            part[:, :, :, columns] = product.astype(BF16).reshape(DEPTH, SIDE, rows_here, tile)
+            return carry
+
+        lax.fori_loop(0, chunk // tile, multiply, 0)
+        x_copy(i).start()
+        if i + 2 < CHUNKS:
+            proj_copy(i + 2).start()
+    for copy in weight_copies:
+        copy.start()
+
+    def head_sum(i):
+        x_copy(i).wait_recv()
+        for d in range(DEPTH):
+            sums[d, :, cuts[i]] = (
+                part[d, x, :, cuts[i]].astype(F32) + x_slots[d, :, cuts[i]].astype(F32)
+            ).astype(BF16)
+        total[:, cuts[i]] = residual[:, cuts[i]].astype(F32) + sums[z, :, cuts[i]].astype(F32)
+        chain_z(place, sums, z_slots, z_send.at[i], z_recv.at[i], cuts[i])
+
+    def index(y, c, z, x):
+        return ((y * 2 + c) * DEPTH + z) * SIDE + x
+
+    mine = index(y, c, z, x)
+    squares = []
+
+    def settle(q):
+        per = CHUNKS // PASSES
+        for i in range(q * per, (q + 1) * per):
+            chain_z_end(place, z_slots, total, z_send.at[i], z_recv.at[i], cuts[i])
+        columns = pl.ds(q * span, span)
+        rounded = total[:, columns].astype(BF16)
+        hidden[:, columns] = rounded
+        wide = rounded.astype(F32)
+        squares.append(jnp.sum(wide * wide, axis=1, keepdims=True))
+        rows[mine, :, columns] = (wide * gain[:, columns]).astype(BF16)
+        if q == PASSES - 1:
+            inverse = lax.rsqrt(sum(squares) / width + 1e-06)
+            high = inverse.astype(BF16).astype(F32)
+            lane = lax.broadcasted_iota(jnp.int32, (rows_here, SIDE_COLUMNS), 1)
+            side = jnp.where(
+                lane == SIDE_COLUMNS - 2, high,
+                jnp.where(lane == SIDE_COLUMNS - 1, inverse - high, weighted[...].astype(F32)),
+            )
+            rows[mine, :, extra] = side.astype(BF16)
+
+    def here(i, by_x, by_y):
+        return index(yo if by_y else y, c, z - OFFSETS[i], xo if by_x else x)
+
+    def copy_to(device, block, q, send, recv):
+        ref = rows.at[block, :, passes[q]]
+        return remote(ref, ref, send, recv, device)
+
+    def z_copy(q, i, step):
+        there = OFFSETS.index(OFFSETS[i] + step)
+        return copy_to(place.at_z(step), here(i, 0, 0), q, a_send.at[q, there], a_recv.at[q, there])
+
+    def z_steps(i):
+        offset = OFFSETS[i]
+        return [s for s in (1, -1) if offset * s >= 0 and abs(offset + s) < DEPTH]
+
+    def x_full(q, i, by_x=0):
+        return copy_to(place.at_x, here(i, by_x, 0), q, b_send.at[q, i, 0], b_recv.at[q, i, 0])
+
+    def y_full(q, i, by_y=0):
+        return copy_to(place.at_y, here(i, 0, by_y), q, b_send.at[q, i, 1], b_recv.at[q, i, 1])
+
+    def y_on(q, i, by_y=0):
+        return copy_to(place.at_y, here(i, 1, by_y), q, d_send.at[q, i], d_recv.at[q, i])
+
+    def core_copy(q, i, by_x, by_y):
+        k = by_x * 2 + by_y
+        return copy_to(place.at_core, here(i, by_x, by_y), q, c_send.at[q, i, k], c_recv.at[q, i, k])
+
+    def core_wait(q, i, by_x, by_y):
+        k = by_x * 2 + by_y
+        block = index(yo if by_y else y, co, z - OFFSETS[i], xo if by_x else x)
+        copy_to(place.at_core, block, q, c_send.at[q, i, k], c_recv.at[q, i, k]).wait_recv()
+
+    def along_z(q, i):
+        def body():
+            if i > 0:
+                copy_to(place.at_x, here(i, 0, 0), q, a_send.at[q, i], a_recv.at[q, i]).wait_recv()
+            for step in z_steps(i):
+                @pl.when(place.has_z(step))
+                def _():
+                    z_copy(q, i, step).start()
+            x_full(q, i).start()
+            y_full(q, i).start()
+            core_copy(q, i, 0, 0).start()
+
+        each(i, body)
+
+    def along_xy(q, i):
+        def body():
+            x_full(q, i, 1).wait_recv()
+            y_on(q, i).start()
+            core_copy(q, i, 1, 0).start()
+            y_full(q, i, 1).wait_recv()
+            core_copy(q, i, 0, 1).start()
+
+        each(i, body)
+
+    def along_diagonal(q, i):
+        def body():
+            y_on(q, i, 1).wait_recv()
+            core_copy(q, i, 1, 1).start()
+
+        each(i, body)
+
+    near = ((0,), (1, 2), (3, 4), (5, 6))
+
+    def level(action, q, t):
+        if 0 <= t < DEPTH:
+            for i in near[t]:
+                action(q, i)
+
+    head_sum(0)
+    head_sum(1)
+    settle(0)
+    level(along_z, 0, 0)
+    head_sum(2)
+    level(along_z, 0, 1)
+    head_sum(3)
+    level(along_xy, 0, 0)
+    settle(1)
+    for t in range(DEPTH + 1):
+        level(along_z, 1, t)
+        level(along_z, 0, t + 2)
+        level(along_xy, 0, t + 1)
+        level(along_xy, 1, t - 1)
+        level(along_diagonal, 0, t)
+        level(along_diagonal, 1, t - 2)
+
+    def all_blocks(action):
+        for q in range(PASSES):
+            for i in range(len(OFFSETS)):
+                each(i, lambda q=q, i=i: action(q, i))
+
+    def cores_near(q, i):
+        core_wait(q, i, 0, 0)
+        core_wait(q, i, 1, 0)
+
+    def cores_far(q, i):
+        core_wait(q, i, 0, 1)
+        core_wait(q, i, 1, 1)
+
+    member_count = SIDE * DEPTH
+    expert = (y * 2 + c) * (member_count // SLICES) + lax.div(z * SIDE + x, SLICES)
+    half_blocks = 2 * DEPTH * SIDE
+
+    def side_of(j):
+        side = rows[pl.ds(j * half_blocks, half_blocks), :, extra].reshape(block_rows, SIDE_COLUMNS)
+        return side.astype(F32), lax.broadcasted_iota(jnp.int32, (block_rows, SIDE_COLUMNS), 1)
+
+    def widen(j):
+        depth = 1024
+
+        def multiply(t, carry):
+            columns = pl.ds(pl.multiple_of(t * depth, depth), depth)
+            block = rows[pl.ds(j * half_blocks, half_blocks), :, columns].reshape(block_rows, depth)
+            return (
+                carry[0] + jnp.dot(block, gate[columns, :], preferred_element_type=F32),
+                carry[1] + jnp.dot(block, up[columns, :], preferred_element_type=F32),
+            )
+
+        zeros = jnp.zeros((block_rows, gate.shape[1]), F32)
+        gate_part, up_part = lax.fori_loop(0, width // depth, multiply, (zeros, zeros))
+        side, lane = side_of(j)
+        inverse = jnp.sum(jnp.where(lane >= SIDE_COLUMNS - 2, side, 0.0), axis=1, keepdims=True)
+        gate_part = gate_part * inverse
+        act[j] = (gate_part / (1.0 + jnp.exp(-gate_part)) * (up_part * inverse)).astype(BF16)
+
+    def narrow(j):
+        side, lane = side_of(j)
+        weight = jnp.sum(jnp.where(lane == expert, side, 0.0), axis=1, keepdims=True)
+        step = 512
+
+        def multiply(t, carry):
+            columns = pl.ds(pl.multiple_of(t * step, step), step)
+            product = jnp.dot(act[j], down[:, columns], preferred_element_type=F32) * weight
+            parts[j, :, :, :, :, columns] = product.astype(BF16).reshape(
+                2, DEPTH, SIDE, rows_here, step
+            )
+            return carry
+
+        lax.fori_loop(0, width // step, multiply, 0)
+
+    for copy in weight_copies:
+        copy.wait()
+    all_blocks(cores_near)
+    widen(y)
+    level(along_diagonal, 1, DEPTH - 1)
+    all_blocks(cores_far)
+    widen(yo)
+
+    half = width // 2
+    cut_a, cut_b, whole = pl.ds(0, half), pl.ds(half, half), pl.ds(0, width)
+    far = (6, 5, 4, 3, 2, 1, 0)
+
+    def part_copy(i, k):
+        d = z - OFFSETS[i]
+        j = (yo, y)[k]
+        return remote(
+            parts.at[j, co, d], core_slots.at[d, j], core_send.at[i, k], core_recv.at[i, k], place.at_core
+        )
+
+    def diagonal_a(i):
+        d = z - OFFSETS[i]
+        return remote(
+            sums2.at[d, yo, xo, :, cut_a], a_slots.at[d], e_send.at[i, 0], e_recv.at[i, 0], place.at_y
+        )
+
+    def diagonal_b(i):
+        d = z - OFFSETS[i]
+        return remote(
+            sums2.at[d, yo, xo, :, cut_b], b_slots.at[d], e_send.at[i, 1], e_recv.at[i, 1], place.at_x
+        )
+
+    def full_x(i):
+        d = z - OFFSETS[i]
+        return remote(sums2.at[d, y, xo], x_slots2.at[d], f_send.at[i, 0], f_recv.at[i, 0], place.at_x)
+
+    def full_y(i):
+        d = z - OFFSETS[i]
+        return remote(sums2.at[d, yo, x], y_slots2.at[d], f_send.at[i, 1], f_recv.at[i, 1], place.at_y)
+
+    def first(i):
+        def body():
+            d = z - OFFSETS[i]
+            for k, j in enumerate((yo, y)):
+                part_copy(i, k).wait_recv()
+                for m in (xo, x):
+                    sums2[d, j, m] = (
+                        parts[j, c, d, m].astype(F32) + core_slots[d, j, m].astype(F32)
+                    ).astype(BF16)
+                    if k == 0 and m is xo:
+                        diagonal_a(i).start()
+                        diagonal_b(i).start()
+
+        each(i, body)
+
+    def second(i):
+        def body():
+            d = z - OFFSETS[i]
+            diagonal_a(i).wait_recv()
+            sums2[d, y, xo, :, cut_a] = (
+                sums2[d, y, xo, :, cut_a].astype(F32) + a_slots[d].astype(F32)
+            ).astype(BF16)
+            full_x(i).start()
+            diagonal_b(i).wait_recv()
+            sums2[d, yo, x, :, cut_b] = (
+                sums2[d, yo, x, :, cut_b].astype(F32) + b_slots[d].astype(F32)
+            ).astype(BF16)
+            full_y(i).start()
+
+        each(i, body)
+
+    def third(i):
+        def body():
+            d = z - OFFSETS[i]
+            full_x(i).wait_recv()
+            full_y(i).wait_recv()
+            own[d] = (
+                sums2[d, y, x].astype(F32) + x_slots2[d].astype(F32) + y_slots2[d].astype(F32)
+            ).astype(BF16)
+
+        each(i, body)
+
+    narrow(yo)
+    for i in far:
+        each(i, lambda i=i: part_copy(i, 0).start())
+    narrow(y)
+    for i in far:
+        each(i, lambda i=i: part_copy(i, 1).start())
+    levels = ((6, 5), (4, 3), (2, 1), (0,))
+    for t in range(len(levels) + 2):
+        for i in levels[t] if t < len(levels) else ():
+            first(i)
+        for i in levels[t - 1] if 0 <= t - 1 < len(levels) else ():
+            second(i)
+        if 0 <= t - 2 < len(levels):
+            for i in levels[t - 2]:
+                third(i)
+            if t - 2 < DEPTH - 1:
+                chain_z(place, own, z_slots2, z2_send, z2_recv, whole, order=(DEPTH - 1 - (t - 2),))
+    out[...] = hidden[...].astype(F32) + own[z].astype(F32)
+    chain_z_end(place, z_slots2, out, z2_send, z2_recv, whole)
+
+    for i in range(CHUNKS):
+        x_copy(i).wait_send()
+        chain_z_sent(place, sums, z_slots, z_send.at[i], z_recv.at[i], cuts[i])
+
+    def sent(q, i):
+        for step in z_steps(i):
+            @pl.when(place.has_z(step))
+            def _():
+                z_copy(q, i, step).wait_send()
+        for copy in (x_full(q, i), y_full(q, i), y_on(q, i)):
+            copy.wait_send()
+        for k in range(4):
+            core_copy(q, i, k // 2, k % 2).wait_send()
+
+    all_blocks(sent)
+    for i in far:
+        def body(i=i):
+            for copy in (
+                part_copy(i, 0), part_copy(i, 1), diagonal_a(i), diagonal_b(i), full_x(i), full_y(i)
+            ):
+                copy.wait_send()
+
+        each(i, body)
+    chain_z_sent(place, own, z_slots2, z2_send, z2_recv, whole)
+
+
+def local_dense(
+    context, out_proj, residual, norm_gain, expert_ids, gates, gate_proj, up_proj, down_proj
+):
+    group_count = lax.axis_size("group")
+    member_count = lax.axis_size("ingroup")
+    devices = group_count * member_count
+    rows, width = residual.shape
+    inner = gate_proj.shape[2]
+    expert_total = group_count * (member_count // SLICES)
+    capacity = min(rows, max(2, rows * TOPK * 5 // (4 * expert_total)))
+    offsets = len(OFFSETS)
+    dma = pltpu.SemaphoreType.DMA
+    vmem = pl.BlockSpec(memory_space=pltpu.VMEM)
+    anywhere = pl.BlockSpec(memory_space=pl.ANY)
+
+    expert_iota = jnp.arange(SIDE_COLUMNS, dtype=jnp.int32)
+    matches = expert_ids[:, :, None] == expert_iota[None, None, :]
+    picked = jnp.any(matches, axis=1).astype(F32)
+    before = jnp.tril(jnp.ones((rows, rows), F32), -1)
+    ranking = jnp.dot(before, picked)
+    weighted = jnp.sum(jnp.where(matches, gates.astype(F32)[:, :, None], F32(0)), axis=1)
+    weighted = jnp.where((picked > 0) & (ranking < capacity), weighted, F32(0)).astype(BF16)
+
+    def half(*shape):
+        return pltpu.VMEM(shape, BF16)
+
+    summed = pl.pallas_call(
+        layer_kernel,
+        out_shape=jax.ShapeDtypeStruct((rows, width), F32),
+        in_specs=[vmem, anywhere, vmem, vmem, vmem, anywhere, anywhere, anywhere],
+        out_specs=vmem,
+        scratch_shapes=[
+            half(2, context.shape[1], width // CHUNKS),
+            half(width, inner), half(width, inner), half(inner, width),
+            half(DEPTH, SIDE, rows, width),
+            half(DEPTH, rows, width),
+            half(DEPTH, rows, width),
+            half(2, DEPTH - 1, rows, width),
+            pltpu.VMEM((rows, width), F32),
+            half(rows, width),
+            half(devices, rows, width + SIDE_COLUMNS),
+            half(SIDE, devices * rows // SIDE, inner),
+            half(SIDE, 2, DEPTH, SIDE, rows, width),
+            half(DEPTH, SIDE, SIDE, rows, width),
+            half(DEPTH, SIDE, SIDE, rows, width),
+            half(DEPTH, rows, width // 2),
+            half(DEPTH, rows, width // 2),
+            half(DEPTH, rows, width),
+            half(DEPTH, rows, width),
+            half(DEPTH, rows, width),
+            half(2, DEPTH - 1, rows, width),
+            dma((3,)), dma((CHUNKS,)),
+            dma((CHUNKS,)), dma((CHUNKS,)),
+            dma((CHUNKS, 2, DEPTH - 1)), dma((CHUNKS, 2, DEPTH - 1)),
+            dma((PASSES, offsets)), dma((PASSES, offsets)),
+            dma((PASSES, offsets, 2)), dma((PASSES, offsets, 2)),
+            dma((PASSES, offsets)), dma((PASSES, offsets)),
+            dma((PASSES, offsets, 4)), dma((PASSES, offsets, 4)),
+            dma((offsets, 2)), dma((offsets, 2)),
+            dma((offsets, 2)), dma((offsets, 2)),
+            dma((offsets, 2)), dma((offsets, 2)),
+            dma((2, DEPTH - 1)), dma((2, DEPTH - 1)),
+        ],
+        compiler_params=pltpu.CompilerParams(
+            collective_id=0, has_side_effects=True, vmem_limit_bytes=58 * 2**20
+        ),
+        name="layer",
+    )(
+        context, out_proj, residual, norm_gain.reshape(1, width), weighted, gate_proj, up_proj,
+        down_proj,
+    )
+    return summed.astype(BF16)
+
+
 def solution(mesh):
     in_specs = (
         P("group", "ingroup"),
@@ -116,4 +634,6 @@
         P(("group", "ingroup"), None, None),
     )
     out_specs = P(("group", "ingroup"), None)
-    return jax.shard_map(local, mesh=mesh, in_specs=in_specs, out_specs=out_specs, check_vma=False)
+    sizes = (mesh.shape["group"], mesh.shape["ingroup"])
+    body = local_dense if sizes == (2 * SIDE, SIDE * DEPTH) else local
+    return jax.shard_map(body, mesh=mesh, in_specs=in_specs, out_specs=out_specs, check_vma=False)

time: 515 us -> 132 us (0.26)
  blocking collectives: 329 us -> 0 us
  Pallas kernels: 0 us -> 128 us
  waiting for transfers between devices: 114 us -> 0 us
  matrix products: 31.9 us -> 0.79 us
  between operations: 13.5 us -> 0.01 us
  starting transfers between devices: 11.3 us -> 0 us
  local copies, waits for them, and re-layouts: 9.76 us -> 1.51 us
    all_to_all x2 -> x0, blocking collectives: 329 us -> none  [the longest x1 165 us: local(): lax.all_to_all(dispatch, 'ingroup', split_axis=0, concat_axis=0, tiled=True)]
    pallas_call x0 -> x1, Pallas kernels: none -> 128 us  [local_dense(): pl.pallas_call(layer_kernel, out_shape=jax.ShapeDtypeStruct((rows, width)...]
    reduce_scatter x1 -> x0, waiting for transfers between devices: 78.1 us -> none  [local(): lax.psum_scatter(jnp.dot(context, out_proj, preferred_element_type=jnp.fl...]
    all_to_all x3 -> x0, waiting for transfers between devices: 35.4 us -> none  [the longest x1 22.7 us: local(): lax.all_to_all(group_out, 'group', split_axis=0, concat_axis=0, tiled=True)]
    dot_general x7 -> x1, matrix products: 31.9 us -> 0.79 us  [local_dense(): ranking = jnp.dot(before, picked)]
    all_to_all x3 -> x0, starting transfers between devices: 11.3 us -> none  [the longest x1 4.24 us: local(): lax.all_to_all(outgoing_gates, 'group', split_axis=0, concat_axis=0, tile...]
  transfers between devices with their start and end apart: 4 -> 0, of which waited for: 3 -> 0; matrix products, arithmetic and copies ran while one was open for 1% -> 0% of each run, Pallas kernels for 0% -> 0%
where the time goes in v2:
time: 132 us
  Pallas kernels  128 us (97%)
  other arithmetic  1.95 us (1%)
  local copies, waits for them, and re-layouts  1.51 us (1%)
    pallas_call x1, Pallas kernels, local_dense(): pl.pallas_call(layer_kernel, out_shape=jax.ShapeDtypeStruct((rows, width)...  128 us

profile of v2, /device:TPU:0, one launch (start us, length us, event | category | flops | bytes accessed | tf_op | source)
XLA Modules:
  0.0 131.8 jit_solution(8322902094740929198)
XLA Ops:
  0.0 0.8 copy.12
  0.8 0.1 fusion.3
  0.9 0.8 copy.13
  1.6 0.1 select_reduce_fusion
  1.7 0.8 fusion.2.weighted
  2.5 127.6 %layer.1 = f32[16,7168]{1,0:T(8,128)} custom-call(bf16[128,1024]{1,0:T(8,128)(2,1)} %context.1, bf16[1024,7168]{1,0:T(8,128)(2,1)} %out_proj.1, bf16[16,7168]{1,0:T(8,128)(2,1)} %residual.1, f32[1,7168]{1,0:T(1,128)} %bitcast.2, bf16[16,128]{1,0:T(8,128)(2,1)} %fusion.2.weighted, bf16[1,7168,256]{2,1,0:T(8,128)(2,1)} %gate_proj.1, ...), custom_call_target="tpu_custom_call" | custom-call | tf_op jit(solution)/shard_map/layer/pallas_call | solution.py:576
  130.1 1.7 %convert_element_type.15 = bf16[16,7168]{1,0:T(8,128)(2,1)} convert(f32[16,7168]{1,0:T(8,128)} %layer.1) | non-fusion elementwise | flops 114688 | bytes 688128 | tf_op jit(solution)/shard_map/convert_element_type | solution.py:621
  (1 shorter events, 0.0 us)

commit v3 on v2

--- a/solution.py
+++ b/solution.py
@@ -135,11 +135,13 @@
     def has_z(self, offset):
         return jnp.logical_and(self.z + offset >= 0, self.z + offset < DEPTH)
 
-    def meet(self):
+    def greet(self):
         barrier = pltpu.get_barrier_semaphore()
         for device in (self.at_x, self.at_y, self.at_core, self.at_z(1), self.at_z(-1)):
             pl.semaphore_signal(barrier, inc=1, device_id=device, device_id_type=MESH)
-        pl.semaphore_wait(barrier, 5)
+
+    def meet(self):
+        pl.semaphore_wait(pltpu.get_barrier_semaphore(), 5)
 
 
 def remote(source, target, send, recv, device):
@@ -189,7 +191,7 @@
 
 
 def layer_kernel(
-    context, out_proj, residual, gain, weighted, gate_proj, up_proj, down_proj, out,
+    capacity, context, out_proj, residual, gain, ids, gates, gate_proj, up_proj, down_proj, out,
     proj, gate, up, down, part, x_slots, sums, z_slots, total, hidden, rows, act, parts,
     core_slots, sums2, a_slots, b_slots, x_slots2, y_slots2, own, z_slots2,
     w_sem, proj_sem, x_send, x_recv, z_send, z_recv,
@@ -218,7 +220,7 @@
     ]
     proj_copy(0).start()
     proj_copy(1).start()
-    place.meet()
+    place.greet()
 
     def x_copy(i):
         return remote(
@@ -237,11 +239,33 @@
             return carry
 
         lax.fori_loop(0, chunk // tile, multiply, 0)
+        if i == 0:
+            place.meet()
         x_copy(i).start()
         if i + 2 < CHUNKS:
             proj_copy(i + 2).start()
     for copy in weight_copies:
         copy.start()
+
+    lane = lax.broadcasted_iota(jnp.int32, (rows_here, SIDE_COLUMNS), 1)
+    down_iota = lax.broadcasted_iota(jnp.int32, (rows_here, rows_here), 0)
+    across_iota = lax.broadcasted_iota(jnp.int32, (rows_here, rows_here), 1)
+
+    def upright(line):
+        spread = jnp.broadcast_to(line, (rows_here, rows_here))
+        return jnp.sum(jnp.where(down_iota == across_iota, spread, 0.0), axis=1, keepdims=True)
+
+    weighted = jnp.zeros((rows_here, SIDE_COLUMNS), F32)
+    picked = jnp.zeros((rows_here, SIDE_COLUMNS), F32)
+    ids_wide, gates_wide = ids[...].astype(F32), gates[...].astype(F32)
+    for j in range(TOPK):
+        match = lane.astype(F32) == upright(ids_wide[j : j + 1, :])
+        weighted += jnp.where(match, upright(gates_wide[j : j + 1, :]), 0.0)
+        picked = jnp.where(match, 1.0, picked)
+    before = jnp.where(down_iota > across_iota, 1.0, 0.0).astype(BF16)
+    ranking = jnp.dot(before, picked.astype(BF16), preferred_element_type=F32)
+    admitted = jnp.where(ranking < capacity, picked, 0.0)
+    weighted = jnp.where(admitted > 0.0, weighted, 0.0)
 
     def head_sum(i):
         x_copy(i).wait_recv()
@@ -250,7 +274,10 @@
                 part[d, x, :, cuts[i]].astype(F32) + x_slots[d, :, cuts[i]].astype(F32)
             ).astype(BF16)
         total[:, cuts[i]] = residual[:, cuts[i]].astype(F32) + sums[z, :, cuts[i]].astype(F32)
-        chain_z(place, sums, z_slots, z_send.at[i], z_recv.at[i], cuts[i])
+        chain(i, 3)
+
+    def chain(i, k):
+        chain_z(place, sums, z_slots, z_send.at[i], z_recv.at[i], cuts[i], order=(k,))
 
     def index(y, c, z, x):
         return ((y * 2 + c) * DEPTH + z) * SIDE + x
@@ -271,10 +298,9 @@
         if q == PASSES - 1:
             inverse = lax.rsqrt(sum(squares) / width + 1e-06)
             high = inverse.astype(BF16).astype(F32)
-            lane = lax.broadcasted_iota(jnp.int32, (rows_here, SIDE_COLUMNS), 1)
             side = jnp.where(
                 lane == SIDE_COLUMNS - 2, high,
-                jnp.where(lane == SIDE_COLUMNS - 1, inverse - high, weighted[...].astype(F32)),
+                jnp.where(lane == SIDE_COLUMNS - 1, inverse - high, weighted),
             )
             rows[mine, :, extra] = side.astype(BF16)
 
@@ -299,8 +325,10 @@
     def y_full(q, i, by_y=0):
         return copy_to(place.at_y, here(i, 0, by_y), q, b_send.at[q, i, 1], b_recv.at[q, i, 1])
 
-    def y_on(q, i, by_y=0):
-        return copy_to(place.at_y, here(i, 1, by_y), q, d_send.at[q, i], d_recv.at[q, i])
+    def onward(q, i, landed=0):
+        device = (place.at_y, place.at_x)[q]
+        block = here(i, 1, 1) if landed else here(i, 1 - q, q)
+        return copy_to(device, block, q, d_send.at[q, i], d_recv.at[q, i])
 
     def core_copy(q, i, by_x, by_y):
         k = by_x * 2 + by_y
@@ -327,17 +355,18 @@
 
     def along_xy(q, i):
         def body():
-            x_full(q, i, 1).wait_recv()
-            y_on(q, i).start()
-            core_copy(q, i, 1, 0).start()
-            y_full(q, i, 1).wait_recv()
-            core_copy(q, i, 0, 1).start()
+            arrivals = [(x_full(q, i, 1), (1, 0)), (y_full(q, i, 1), (0, 1))]
+            for n in (q, 1 - q):
+                arrivals[n][0].wait_recv()
+                if n == q:
+                    onward(q, i).start()
+                core_copy(q, i, *arrivals[n][1]).start()
 
         each(i, body)
 
     def along_diagonal(q, i):
         def body():
-            y_on(q, i, 1).wait_recv()
+            onward(q, i, 1).wait_recv()
             core_copy(q, i, 1, 1).start()
 
         each(i, body)
@@ -350,13 +379,21 @@
                 action(q, i)
 
     head_sum(0)
+    chain(0, 2)
     head_sum(1)
+    chain(0, 1)
+    chain(1, 2)
+    head_sum(2)
+    chain(1, 1)
+    chain(2, 2)
     settle(0)
     level(along_z, 0, 0)
-    head_sum(2)
+    head_sum(3)
+    chain(2, 1)
+    chain(3, 2)
     level(along_z, 0, 1)
-    head_sum(3)
     level(along_xy, 0, 0)
+    chain(3, 1)
     settle(1)
     for t in range(DEPTH + 1):
         level(along_z, 1, t)
@@ -459,18 +496,18 @@
         d = z - OFFSETS[i]
         return remote(sums2.at[d, yo, x], y_slots2.at[d], f_send.at[i, 1], f_recv.at[i, 1], place.at_y)
 
-    def first(i):
+    def first(i, k):
         def body():
             d = z - OFFSETS[i]
-            for k, j in enumerate((yo, y)):
-                part_copy(i, k).wait_recv()
-                for m in (xo, x):
-                    sums2[d, j, m] = (
-                        parts[j, c, d, m].astype(F32) + core_slots[d, j, m].astype(F32)
-                    ).astype(BF16)
-                    if k == 0 and m is xo:
-                        diagonal_a(i).start()
-                        diagonal_b(i).start()
+            j = (yo, y)[k]
+            part_copy(i, k).wait_recv()
+            for m in (xo, x):
+                sums2[d, j, m] = (
+                    parts[j, c, d, m].astype(F32) + core_slots[d, j, m].astype(F32)
+                ).astype(BF16)
+                if k == 0 and m is xo:
+                    diagonal_a(i).start()
+                    diagonal_b(i).start()
 
         each(i, body)
 
@@ -504,13 +541,15 @@
     narrow(yo)
     for i in far:
         each(i, lambda i=i: part_copy(i, 0).start())
+    for i in far:
+        first(i, 0)
     narrow(y)
     for i in far:
         each(i, lambda i=i: part_copy(i, 1).start())
     levels = ((6, 5), (4, 3), (2, 1), (0,))
     for t in range(len(levels) + 2):
         for i in levels[t] if t < len(levels) else ():
-            first(i)
+            first(i, 1)
         for i in levels[t - 1] if 0 <= t - 1 < len(levels) else ():
             second(i)
         if 0 <= t - 2 < len(levels):
@@ -518,8 +557,9 @@
                 third(i)
             if t - 2 < DEPTH - 1:
                 chain_z(place, own, z_slots2, z2_send, z2_recv, whole, order=(DEPTH - 1 - (t - 2),))
-    out[...] = hidden[...].astype(F32) + own[z].astype(F32)
-    chain_z_end(place, z_slots2, out, z2_send, z2_recv, whole)
+    total[...] = hidden[...].astype(F32) + own[z].astype(F32)
+    chain_z_end(place, z_slots2, total, z2_send, z2_recv, whole)
+    out[...] = total[...].astype(BF16)
 
     for i in range(CHUNKS):
         x_copy(i).wait_send()
@@ -530,7 +570,7 @@
             @pl.when(place.has_z(step))
             def _():
                 z_copy(q, i, step).wait_send()
-        for copy in (x_full(q, i), y_full(q, i), y_on(q, i)):
+        for copy in (x_full(q, i), y_full(q, i), onward(q, i)):
             copy.wait_send()
         for k in range(4):
             core_copy(q, i, k // 2, k % 2).wait_send()
@@ -562,21 +602,13 @@
     vmem = pl.BlockSpec(memory_space=pltpu.VMEM)
     anywhere = pl.BlockSpec(memory_space=pl.ANY)
 
-    expert_iota = jnp.arange(SIDE_COLUMNS, dtype=jnp.int32)
-    matches = expert_ids[:, :, None] == expert_iota[None, None, :]
-    picked = jnp.any(matches, axis=1).astype(F32)
-    before = jnp.tril(jnp.ones((rows, rows), F32), -1)
-    ranking = jnp.dot(before, picked)
-    weighted = jnp.sum(jnp.where(matches, gates.astype(F32)[:, :, None], F32(0)), axis=1)
-    weighted = jnp.where((picked > 0) & (ranking < capacity), weighted, F32(0)).astype(BF16)
-
     def half(*shape):
         return pltpu.VMEM(shape, BF16)
 
-    summed = pl.pallas_call(
-        layer_kernel,
-        out_shape=jax.ShapeDtypeStruct((rows, width), F32),
-        in_specs=[vmem, anywhere, vmem, vmem, vmem, anywhere, anywhere, anywhere],
+    return pl.pallas_call(
+        functools.partial(layer_kernel, capacity),
+        out_shape=jax.ShapeDtypeStruct((rows, width), BF16),
+        in_specs=[vmem, anywhere, vmem, vmem, vmem, vmem, anywhere, anywhere, anywhere],
         out_specs=vmem,
         scratch_shapes=[
             half(2, context.shape[1], width // CHUNKS),
@@ -615,10 +647,9 @@
         ),
         name="layer",
     )(
-        context, out_proj, residual, norm_gain.reshape(1, width), weighted, gate_proj, up_proj,
-        down_proj,
-    )
-    return summed.astype(BF16)
+        context, out_proj, residual, norm_gain.reshape(1, width), expert_ids.T, gates.T, gate_proj,
+        up_proj, down_proj,
+    )
 
 
 def solution(mesh):

time: 132 us -> 118 us (0.89)
  Pallas kernels: 128 us -> 116 us
  other arithmetic: 1.95 us -> 0 us
    pallas_call x1, Pallas kernels: 128 us -> 116 us  [local_dense(): pl.pallas_call(functools.partial(layer_kernel, capacity), out_shape=jax.S...]
    convert_element_type x1 -> x0, other arithmetic: 1.73 us -> none  [local_dense(): return summed.astype(BF16)]
where the time goes in v3:
time: 118 us
  Pallas kernels  116 us (98%)
  local copies, waits for them, and re-layouts  1.64 us (1%)
    pallas_call x1, Pallas kernels, local_dense(): pl.pallas_call(functools.partial(layer_kernel, capacity), out_shape=jax.S...  116 us

profile of v3, /device:TPU:0, one launch (start us, length us, event | category | flops | bytes accessed | tf_op | source)
XLA Modules:
  0.0 117.9 jit_solution(5872726126321126048)
XLA Ops:
  0.0 116.2 %layer.1 = bf16[16,7168]{1,0:T(8,128)(2,1)} custom-call(bf16[128,1024]{1,0:T(8,128)(2,1)} %context.1, bf16[1024,7168]{1,0:T(8,128)(2,1)} %out_proj.1, bf16[16,7168]{1,0:T(8,128)(2,1)} %residual.1, f32[1,7168]{1,0:T(1,128)} %bitcast.3, s32[8,16]{1,0:T(8,128)} %bitcast.4, bf16[8,16]{1,0:T(8,128)(2,1)} %bitcast.5, bf16[1,7168,256]{2,1,0:T(8,128)(2,1)} %gate_proj.1, ...), custom_call_target="tpu_custom_call" | custom-call | tf_op jit(solution)/shard_map/layer/pallas_call | solution.py:608
  116.2 1.6 %copy.11 = bf16[16,7168]{1,0:T(8,128)(2,1)} copy(bf16[16,7168]{1,0:T(8,128)(2,1)} %layer.1) | data formatting | bytes 458752

commit v4 on v3

--- a/solution.py
+++ b/solution.py
@@ -110,7 +110,6 @@
 SIDE = 2
 DEPTH = 4
 CHUNKS = 4
-PASSES = 2
 SIDE_COLUMNS = 128
 OFFSETS = (0, 1, -1, 2, -2, 3, -3)
 MESH = pl.DeviceIdType.MESH
@@ -202,11 +201,11 @@
     x, y, z, c, xo, yo, co = place.x, place.y, place.z, place.c, place.xo, place.yo, place.co
     rows_here, width = residual.shape
     chunk = width // CHUNKS
-    span = width // PASSES
     block_rows = rows_here * SIDE * 2 * DEPTH
     cuts = [pl.ds(i * chunk, chunk) for i in range(CHUNKS)]
     extra = pl.ds(width, SIDE_COLUMNS)
-    passes = [pl.ds(0, span), pl.ds(span, span + SIDE_COLUMNS)]
+    last = CHUNKS - 1
+    passes = cuts[:last] + [pl.ds(last * chunk, chunk + SIDE_COLUMNS)]
 
     def each(i, body):
         pl.when(place.has_z(-OFFSETS[i]))(body)
@@ -274,7 +273,7 @@
                 part[d, x, :, cuts[i]].astype(F32) + x_slots[d, :, cuts[i]].astype(F32)
             ).astype(BF16)
         total[:, cuts[i]] = residual[:, cuts[i]].astype(F32) + sums[z, :, cuts[i]].astype(F32)
-        chain(i, 3)
+        chain(i, DEPTH - 1)
 
     def chain(i, k):
         chain_z(place, sums, z_slots, z_send.at[i], z_recv.at[i], cuts[i], order=(k,))
@@ -286,16 +285,14 @@
     squares = []
 
     def settle(q):
-        per = CHUNKS // PASSES
-        for i in range(q * per, (q + 1) * per):
-            chain_z_end(place, z_slots, total, z_send.at[i], z_recv.at[i], cuts[i])
-        columns = pl.ds(q * span, span)
+        columns = cuts[q]
+        chain_z_end(place, z_slots, total, z_send.at[q], z_recv.at[q], columns)
         rounded = total[:, columns].astype(BF16)
         hidden[:, columns] = rounded
         wide = rounded.astype(F32)
         squares.append(jnp.sum(wide * wide, axis=1, keepdims=True))
         rows[mine, :, columns] = (wide * gain[:, columns]).astype(BF16)
-        if q == PASSES - 1:
+        if q == last:
             inverse = lax.rsqrt(sum(squares) / width + 1e-06)
             high = inverse.astype(BF16).astype(F32)
             side = jnp.where(
@@ -325,9 +322,12 @@
     def y_full(q, i, by_y=0):
         return copy_to(place.at_y, here(i, 0, by_y), q, b_send.at[q, i, 1], b_recv.at[q, i, 1])
 
+    def route(q):
+        return q * 2 // CHUNKS
+
     def onward(q, i, landed=0):
-        device = (place.at_y, place.at_x)[q]
-        block = here(i, 1, 1) if landed else here(i, 1 - q, q)
+        device = (place.at_y, place.at_x)[route(q)]
+        block = here(i, 1, 1) if landed else here(i, 1 - route(q), route(q))
         return copy_to(device, block, q, d_send.at[q, i], d_recv.at[q, i])
 
     def core_copy(q, i, by_x, by_y):
@@ -356,9 +356,9 @@
     def along_xy(q, i):
         def body():
             arrivals = [(x_full(q, i, 1), (1, 0)), (y_full(q, i, 1), (0, 1))]
-            for n in (q, 1 - q):
+            for n in (route(q), 1 - route(q)):
                 arrivals[n][0].wait_recv()
-                if n == q:
+                if n == route(q):
                     onward(q, i).start()
                 core_copy(q, i, *arrivals[n][1]).start()
 
@@ -378,33 +378,29 @@
             for i in near[t]:
                 action(q, i)
 
-    head_sum(0)
-    chain(0, 2)
-    head_sum(1)
-    chain(0, 1)
-    chain(1, 2)
-    head_sum(2)
-    chain(1, 1)
-    chain(2, 2)
-    settle(0)
-    level(along_z, 0, 0)
-    head_sum(3)
-    chain(2, 1)
-    chain(3, 2)
-    level(along_z, 0, 1)
-    level(along_xy, 0, 0)
-    chain(3, 1)
-    settle(1)
-    for t in range(DEPTH + 1):
-        level(along_z, 1, t)
-        level(along_z, 0, t + 2)
-        level(along_xy, 0, t + 1)
-        level(along_xy, 1, t - 1)
-        level(along_diagonal, 0, t)
-        level(along_diagonal, 1, t - 2)
+    def stage(q, s):
+        if s == 0:
+            head_sum(q)
+        elif s < DEPTH - 1:
+            chain(q, DEPTH - 1 - s)
+        elif s == DEPTH - 1:
+            settle(q)
+            level(along_z, q, 0)
+        else:
+            t = s - (DEPTH - 1)
+            level(along_z, q, t)
+            level(along_xy, q, t - 1)
+            if (q, t - 2) != (last, DEPTH - 1):
+                level(along_diagonal, q, t - 2)
+
+    stages = 2 * DEPTH + 1
+    for s in range(2 * last + stages):
+        for q in range(CHUNKS):
+            if 0 <= s - 2 * q < stages:
+                stage(q, s - 2 * q)
 
     def all_blocks(action):
-        for q in range(PASSES):
+        for q in range(CHUNKS):
             for i in range(len(OFFSETS)):
                 each(i, lambda q=q, i=i: action(q, i))
 
@@ -461,7 +457,7 @@
         copy.wait()
     all_blocks(cores_near)
     widen(y)
-    level(along_diagonal, 1, DEPTH - 1)
+    level(along_diagonal, last, DEPTH - 1)
     all_blocks(cores_far)
     widen(yo)
 
@@ -633,10 +629,10 @@
             dma((3,)), dma((CHUNKS,)),
             dma((CHUNKS,)), dma((CHUNKS,)),
             dma((CHUNKS, 2, DEPTH - 1)), dma((CHUNKS, 2, DEPTH - 1)),
-            dma((PASSES, offsets)), dma((PASSES, offsets)),
-            dma((PASSES, offsets, 2)), dma((PASSES, offsets, 2)),
-            dma((PASSES, offsets)), dma((PASSES, offsets)),
-            dma((PASSES, offsets, 4)), dma((PASSES, offsets, 4)),
+            dma((CHUNKS, offsets)), dma((CHUNKS, offsets)),
+            dma((CHUNKS, offsets, 2)), dma((CHUNKS, offsets, 2)),
+            dma((CHUNKS, offsets)), dma((CHUNKS, offsets)),
+            dma((CHUNKS, offsets, 4)), dma((CHUNKS, offsets, 4)),
             dma((offsets, 2)), dma((offsets, 2)),
             dma((offsets, 2)), dma((offsets, 2)),
             dma((offsets, 2)), dma((offsets, 2)),

time: 118 us -> 127 us (1.076)
  Pallas kernels: 116 us -> 125 us
    pallas_call x1, Pallas kernels: 116 us -> 125 us  [local_dense(): pl.pallas_call(functools.partial(layer_kernel, capacity), out_shape=jax.S...]
where the time goes in v4:
time: 127 us
  Pallas kernels  125 us (98%)
  local copies, waits for them, and re-layouts  1.64 us (1%)
    pallas_call x1, Pallas kernels, local_dense(): pl.pallas_call(functools.partial(layer_kernel, capacity), out_shape=jax.S...  125 us

profile of v4, /device:TPU:0, one launch (start us, length us, event | category | flops | bytes accessed | tf_op | source)
XLA Modules:
  0.0 126.5 jit_solution(4327490520225300361)
XLA Ops:
  0.0 124.9 %layer.1 = bf16[16,7168]{1,0:T(8,128)(2,1)} custom-call(bf16[128,1024]{1,0:T(8,128)(2,1)} %context.1, bf16[1024,7168]{1,0:T(8,128)(2,1)} %out_proj.1, bf16[16,7168]{1,0:T(8,128)(2,1)} %residual.1, f32[1,7168]{1,0:T(1,128)} %bitcast.3, s32[8,16]{1,0:T(8,128)} %bitcast.4, bf16[8,16]{1,0:T(8,128)(2,1)} %bitcast.5, bf16[1,7168,256]{2,1,0:T(8,128)(2,1)} %gate_proj.1, ...), custom_call_target="tpu_custom_call" | custom-call | tf_op jit(solution)/shard_map/layer/pallas_call | solution.py:604
  124.9 1.6 %copy.11 = bf16[16,7168]{1,0:T(8,128)(2,1)} copy(bf16[16,7168]{1,0:T(8,128)(2,1)} %layer.1) | data formatting | bytes 458752

commit v5 on v3

--- a/solution.py
+++ b/solution.py
@@ -330,14 +330,9 @@
         block = here(i, 1, 1) if landed else here(i, 1 - q, q)
         return copy_to(device, block, q, d_send.at[q, i], d_recv.at[q, i])
 
-    def core_copy(q, i, by_x, by_y):
-        k = by_x * 2 + by_y
-        return copy_to(place.at_core, here(i, by_x, by_y), q, c_send.at[q, i, k], c_recv.at[q, i, k])
-
-    def core_wait(q, i, by_x, by_y):
-        k = by_x * 2 + by_y
-        block = index(yo if by_y else y, co, z - OFFSETS[i], xo if by_x else x)
-        copy_to(place.at_core, block, q, c_send.at[q, i, k], c_recv.at[q, i, k]).wait_recv()
+    def core_copy(q, i, by_y, owner):
+        pair = pl.ds(index(yo if by_y else y, owner, z - OFFSETS[i], 0), SIDE)
+        return copy_to(place.at_core, pair, q, c_send.at[q, i, by_y], c_recv.at[q, i, by_y])
 
     def along_z(q, i):
         def body():
@@ -349,25 +344,23 @@
                     z_copy(q, i, step).start()
             x_full(q, i).start()
             y_full(q, i).start()
-            core_copy(q, i, 0, 0).start()
 
         each(i, body)
 
     def along_xy(q, i):
         def body():
-            arrivals = [(x_full(q, i, 1), (1, 0)), (y_full(q, i, 1), (0, 1))]
-            for n in (q, 1 - q):
-                arrivals[n][0].wait_recv()
-                if n == q:
-                    onward(q, i).start()
-                core_copy(q, i, *arrivals[n][1]).start()
+            arrivals = (x_full(q, i, 1), y_full(q, i, 1))
+            arrivals[q].wait_recv()
+            onward(q, i).start()
+            arrivals[1 - q].wait_recv()
+            core_copy(q, i, 0, c).start()
 
         each(i, body)
 
     def along_diagonal(q, i):
         def body():
             onward(q, i, 1).wait_recv()
-            core_copy(q, i, 1, 1).start()
+            core_copy(q, i, 1, c).start()
 
         each(i, body)
 
@@ -409,12 +402,10 @@
                 each(i, lambda q=q, i=i: action(q, i))
 
     def cores_near(q, i):
-        core_wait(q, i, 0, 0)
-        core_wait(q, i, 1, 0)
+        core_copy(q, i, 0, co).wait_recv()
 
     def cores_far(q, i):
-        core_wait(q, i, 0, 1)
-        core_wait(q, i, 1, 1)
+        core_copy(q, i, 1, co).wait_recv()
 
     member_count = SIDE * DEPTH
     expert = (y * 2 + c) * (member_count // SLICES) + lax.div(z * SIDE + x, SLICES)
@@ -572,8 +563,8 @@
                 z_copy(q, i, step).wait_send()
         for copy in (x_full(q, i), y_full(q, i), onward(q, i)):
             copy.wait_send()
-        for k in range(4):
-            core_copy(q, i, k // 2, k % 2).wait_send()
+        for by_y in (0, 1):
+            core_copy(q, i, by_y, c).wait_send()
 
     all_blocks(sent)
     for i in far:
@@ -636,7 +627,7 @@
             dma((PASSES, offsets)), dma((PASSES, offsets)),
             dma((PASSES, offsets, 2)), dma((PASSES, offsets, 2)),
             dma((PASSES, offsets)), dma((PASSES, offsets)),
-            dma((PASSES, offsets, 4)), dma((PASSES, offsets, 4)),
+            dma((PASSES, offsets, 2)), dma((PASSES, offsets, 2)),
             dma((offsets, 2)), dma((offsets, 2)),
             dma((offsets, 2)), dma((offsets, 2)),
             dma((offsets, 2)), dma((offsets, 2)),

time: 118 us -> 118 us (level)
  no operation moved by 1% of the time
where the time goes in v5:
time: 118 us
  Pallas kernels  117 us (99%)
  local copies, waits for them, and re-layouts  1.64 us (1%)
    pallas_call x1, Pallas kernels, local_dense(): pl.pallas_call(functools.partial(layer_kernel, capacity), out_shape=jax.S...  117 us

profile of v5, /device:TPU:0, one launch (start us, length us, event | category | flops | bytes accessed | tf_op | source)
XLA Modules:
  0.0 118.3 jit_solution(591678983922398524)
XLA Ops:
  0.0 116.6 %layer.1 = bf16[16,7168]{1,0:T(8,128)(2,1)} custom-call(bf16[128,1024]{1,0:T(8,128)(2,1)} %context.1, bf16[1024,7168]{1,0:T(8,128)(2,1)} %out_proj.1, bf16[16,7168]{1,0:T(8,128)(2,1)} %residual.1, f32[1,7168]{1,0:T(1,128)} %bitcast.3, s32[8,16]{1,0:T(8,128)} %bitcast.4, bf16[8,16]{1,0:T(8,128)(2,1)} %bitcast.5, bf16[1,7168,256]{2,1,0:T(8,128)(2,1)} %gate_proj.1, ...), custom_call_target="tpu_custom_call" | custom-call | tf_op jit(solution)/shard_map/layer/pallas_call | solution.py:599
  116.6 1.6 %copy.11 = bf16[16,7168]{1,0:T(8,128)(2,1)} copy(bf16[16,7168]{1,0:T(8,128)(2,1)} %layer.1) | data formatting | bytes 458752
